TPU v7x, 512 devices: a whole 4x4x16 slice. The times are simulated.
512 devices in a mesh: grp: 16 (over z), row: 32 (over y, x, core).
Axes of the slice: x: 4, y: 4, z: 16, core: 2. Of those that a mesh axis runs over, the one named last changes fastest.
Arguments:
- features: bfloat16 [131072, 1024], P(('grp', 'row')), may hold values from -6 to 6
- history: bfloat16 [196608, 1024], P(('grp', 'row')), may hold values from -6 to 6
- weight: bfloat16 [1024, 1024], replicated, may hold values from -3 to 3
- in_tiles: bfloat16 [16, 64, 8, 128, 128], P('grp', 'row'), may hold values from 0 to 9, as said below
- in_cols: int32 [16, 64, 8], P('grp', 'row'), may hold values from 0 to 63, as said below
- tile_live: int32 [16, 64], P('grp', 'row'), may hold values from 1 to 8, 341 in all within a row
- hist_tiles: bfloat16 [16, 64, 8, 128, 128], P('grp', 'row'), may hold values from 0 to 9, as said below
- hist_owner: int32 [8192, 1], P(('grp', 'row')), may hold values from 0 to 15; in each aligned block of 16 rows (0 to 15, 16 to 31, ...) at most 2 rows name the same one
- hist_block: int32 [8192, 1], P(('grp', 'row')), may hold values from 0 to 2
Outputs:
- node_out: bfloat16 [131072, 1024], P(('grp', 'row'))
Inputs may be any that keep to these rules, and one draw needn't show every extreme that they name: `in_cols`: slot t of row block b names a column block of the same group within 6 blocks of b; slot 0 names b itself, the other slots distinct offsets, cut to the group's blocks at its ends. Only the first tile_live slots of a row block are tiles of the graph; a group's counts sum to 341. `hist_owner`: among the 16 requests of one device's rows at most 2 name one group, a bound that some block reaches. `in_tiles`: Positive. `hist_tiles`: Positive.
All inputs are finite; a program needn't handle non-finite values.
Results may differ from a plain program's by a relative error of at most 0.0049.
Values may be sent and summed in bfloat16 or wider, within the bound.
A program may use at most 128 MiB of HBM per device.

v0:
```python
import jax
import jax.numpy as jnp
from jax import lax
from jax.sharding import PartitionSpec as P

BAND = 6


def shifted_2(value, axis, steps):
    count = lax.axis_size(axis)
    initial, last = (max(0, -steps), min(count, count - steps))
    return lax.ppermute(value, axis, [(source, source + steps) for source in range(initial, last)])


def copy_blocks(buffer, piece, wanted_rows, tile_size):
    piece_rows = piece.shape[0]
    inside = (wanted_rows >= 0) & (wanted_rows + tile_size <= piece_rows)
    clipped = jnp.clip(wanted_rows, 0, piece_rows - tile_size)

    def take_block(offset):
        return lax.dynamic_slice_in_dim(piece, offset, tile_size, 0)

    fetched = jax.vmap(take_block)(clipped)
    return jnp.where(inside.reshape(inside.shape + (1, 1)), fetched, buffer)


def body(
    features, history, weight, in_tiles, in_cols, tile_live, hist_tiles, hist_owner, hist_block
):
    tile_size = in_tiles.shape[3]
    feat_width = features.shape[1]
    row_count = features.shape[0]
    block_count = row_count // tile_size
    slot_count = in_tiles.shape[2]
    far_count = hist_tiles.shape[2]
    column_ids = in_cols[0]
    live_counts = tile_live[0]
    near_vals = in_tiles[0]
    far_vals = hist_tiles[0]
    owner_ids = hist_owner[:, 0]
    local_ids = hist_block[:, 0]
    request_count = owner_ids.shape[0]
    hist_blocks = history.reshape(-1, tile_size, feat_width)
    reach_dev = (BAND + block_count - 1) // block_count
    distances = [step_size for step_size in range(reach_dev, -reach_dev - 1, -1) if step_size != 0]
    shifted = {}
    for distance in distances:
        shifted[distance] = shifted_2(features, "row", distance)
    window = jnp.concatenate(
        [
            shifted[step_size] if step_size != 0 else features
            for step_size in range(reach_dev, -reach_dev - 1, -1)
        ],
        axis=0,
    )
    window_blocks = window.reshape(-1, tile_size, feat_width)
    first_block = (lax.axis_index("row") - reach_dev) * block_count
    near_rows = window_blocks[column_ids - first_block]
    empty_far = jnp.zeros((request_count, tile_size, feat_width), jnp.bfloat16)
    wanted_rows = (owner_ids * hist_blocks.shape[0] + local_ids) * tile_size
    far_rows = copy_blocks(
        empty_far, lax.all_gather(history, "grp", axis=0, tiled=True), wanted_rows, tile_size
    )
    far_rows = far_rows.reshape(block_count, far_count, tile_size, feat_width)

    def block_mean(block_index):
        near_tiles = near_vals[block_index]
        near_data = near_rows[block_index]
        far_tiles = far_vals[block_index]
        far_data = far_rows[block_index]
        live_here = live_counts[block_index]

        def add_tile(position, totals):
            return totals + jnp.dot(
                near_tiles[position], near_data[position], preferred_element_type=jnp.float32
            )

        totals = lax.fori_loop(
            0, live_here, add_tile, jnp.zeros((tile_size, feat_width), jnp.float32)
        )
        totals = totals + jnp.einsum(
            "hij,hjd->id", far_tiles, far_data, preferred_element_type=jnp.float32
        )
        is_live = jnp.arange(slot_count, dtype=jnp.int32) < live_here
        near_sums = jnp.sum(
            jnp.where(is_live[:, None, None], near_tiles.astype(jnp.float32), 0.0), axis=(0, 2)
        )
        weight_sums = near_sums + jnp.sum(far_tiles.astype(jnp.float32), axis=(0, 2))
        return (totals / weight_sums[:, None]).astype(jnp.bfloat16)

    mean_rows = lax.map(block_mean, jnp.arange(block_count, dtype=jnp.int32)).reshape(
        row_count, feat_width
    )
    return jax.nn.relu(jnp.dot(mean_rows, weight, preferred_element_type=jnp.float32)).astype(
        jnp.bfloat16
    )


def solution(mesh):
    placed = (
        P(("grp", "row"), None),
        P(("grp", "row"), None),
        P(),
        P("grp", "row", None, None, None),
        P("grp", "row", None),
        P("grp", "row"),
        P("grp", "row", None, None, None),
        P(("grp", "row"), None),
        P(("grp", "row"), None),
    )
    return jax.shard_map(
        body, mesh=mesh, in_specs=placed, out_specs=P(("grp", "row"), None), check_vma=False
    )
```

profile of v0, /device:TPU:3, one launch (start us, length us, event | category | flops | bytes accessed | tf_op | source)
XLA Modules:
  0.0 276.5 jit_solution(2639740686505517836)
XLA Ops:
  7.3 4.4 %collective-permute-start = (bf16[256,1024]{1,0:T(8,128)(2,1)}, bf16[256,1024]{1,0:T(8,128)(2,1)}, u32[]{:S(2)}, u32[]{:S(2)}) collective-permute-start(bf16[256,1024]{1,0:T(8,128)(2,1)} %param.13), channel_id=1, source_target_pairs={{0,3},{1,4},{2,5},{3,6},{4,7},{5,8},{6,9},{7,10},{8,11},{9,12},{10... | collective-permute-start | bytes 1572872 | tf_op jit(solution)/shard_map/ppermute | solution.py:12
  11.7 2.5 collective-permute-start.1
  14.2 2.8 %collective-permute-start.2 = (bf16[256,1024]{1,0:T(8,128)(2,1)}, bf16[256,1024]{1,0:T(8,128)(2,1)}, u32[]{:S(2)}, u32[]{:S(2)}) collective-permute-start(bf16[256,1024]{1,0:T(8,128)(2,1)} %param.13), channel_id=1, source_target_pairs={{0,1},{1,2},{2,3},{3,4},{4,5},{5,6},{6,7},{7,8},{8,9},{9,10},{10,1... | collective-permute-start | bytes 1572872 | tf_op jit(solution)/shard_map/ppermute | solution.py:12
  19.0 4.8 %collective-permute-start.4 = (bf16[256,1024]{1,0:T(8,128)(2,1)}, bf16[256,1024]{1,0:T(8,128)(2,1)S(1)}, u32[]{:S(2)}, u32[]{:S(2)}) collective-permute-start(bf16[256,1024]{1,0:T(8,128)(2,1)} %param.13), channel_id=1, source_target_pairs={{2,0},{3,1},{4,2},{5,3},{6,4},{7,5},{8,6},{9,7},{10,8},{11,9},{12,... | collective-permute-start | bytes 1572872 | tf_op jit(solution)/shard_map/ppermute | solution.py:12
  31.5 3.1 %collective-permute-done.1 = bf16[256,1024]{1,0:T(8,128)(2,1)} collective-permute-done((bf16[256,1024]{1,0:T(8,128)(2,1)}, bf16[256,1024]{1,0:T(8,128)(2,1)}, u32[]{:S(2)}, u32[]{:S(2)}) %collective-permute-start.1) | collective-permute-done | bytes 524320 | tf_op jit(solution)/shard_map/ppermute | solution.py:12
  36.5 3.5 %collective-permute-done.2 = bf16[256,1024]{1,0:T(8,128)(2,1)} collective-permute-done((bf16[256,1024]{1,0:T(8,128)(2,1)}, bf16[256,1024]{1,0:T(8,128)(2,1)}, u32[]{:S(2)}, u32[]{:S(2)}) %collective-permute-start.2) | collective-permute-done | bytes 524320 | tf_op jit(solution)/shard_map/ppermute | solution.py:12
  45.4 6.3 %collective-permute-done.5 = bf16[256,1024]{1,0:T(8,128)(2,1)S(1)} collective-permute-done((bf16[256,1024]{1,0:T(8,128)(2,1)}, bf16[256,1024]{1,0:T(8,128)(2,1)S(1)}, u32[]{:S(2)}, u32[]{:S(2)}) %collective-permute-start.5) | collective-permute-done | bytes 524320 | tf_op jit(solution)/shard_map/ppermute | solution.py:12
  52.6 4.8 %gather_fusion = bf16[16,128,1024]{2,1,0:T(8,128)(2,1)} fusion(bf16[14,128,1024]{2,1,0:T(8,128)(2,1)} %bitcast.12, s32[1024]{0:T(1024)S(1)} %pad_clamp_fusion), kind=kCustom, calls=%fused_computation | custom fusion | bytes 8388672 | tf_op jit(solution)/shard_map/gather | solution.py:58
  57.4 104.6 %all-gather.2.cloned.1.call-done = bf16[6144,1024]{1,0:T(8,128)(2,1)} async-done(((bf16[384,1024]{1,0:T(8,128)(2,1)}), bf16[6144,1024]{1,0:T(8,128)(2,1)}) %all-gather.2.cloned.1.call-update) | async-done | bytes 12582928 | tf_op jit(solution)/shard_map/all_gather | solution.py:62
  162.0 48.3 %while.23 = (s32[]{:T(128)}, bf16[6144,1024]{1,0:T(8,128)(2,1)}, s32[16,2]{0,1:T(2,128)S(1)}, bf16[16,128,1024]{2,1,0:T(8,128)(2,1)}, s32[]{:T(128)}) while((s32[]{:T(128)}, bf16[6144,1024]{1,0:T(8,128)(2,1)}, s32[16,2]{0,1:T(2,128)S(1)}, bf16[16,128,1024]{2,1,0:T(8,128)(2,1)}, s32[]{:T(128)}) %tuple.52), condition=%wide.while_cond, body=%wide.while_body.sunk | while | flops 2 | bytes 525401 | solution.py:21
  162.6 2.4 bitcast_dynamic-update-slice_fusion.2
  165.7 2.4 bitcast_dynamic-update-slice_fusion.2
  168.7 2.4 bitcast_dynamic-update-slice_fusion.2
  174.7 2.4 bitcast_dynamic-update-slice_fusion.2
  177.8 2.4 bitcast_dynamic-update-slice_fusion.2
  180.8 2.4 bitcast_dynamic-update-slice_fusion.2
  183.8 2.4 bitcast_dynamic-update-slice_fusion.2
  186.8 2.4 bitcast_dynamic-update-slice_fusion.2
  189.8 2.4 bitcast_dynamic-update-slice_fusion.2
  192.8 2.4 bitcast_dynamic-update-slice_fusion.2
  195.9 2.4 bitcast_dynamic-update-slice_fusion.2
  198.9 2.4 bitcast_dynamic-update-slice_fusion.2
  201.9 2.4 bitcast_dynamic-update-slice_fusion.2
  210.3 4.5 %broadcast_select_fusion = bf16[2,8,128,1024]{3,2,1,0:T(8,128)(2,1)} fusion(bf16[2,8,128,1024]{3,2,1,0:T(8,128)(2,1)} %bitcast.87, pred[2,8]{1,0:T(4,128)(4,1)S(1)} %reshape.88), kind=kLoop, calls=%fused_computation.26 | loop fusion | flops 2097152 | bytes 8388624 | tf_op jit(solution)/shard_map/jit(_where)/select_n | solution.py:24
  214.8 52.3 %while.22 = (s32[]{:T(128)}, bf16[2,128,1024]{2,1,0:T(8,128)(2,1)}, s32[2]{0:T(128)S(1)}, s32[2]{0:T(128)S(1)}, bf16[2,8,128,128]{3,2,1,0:T(8,128)(2,1)S(1)}, /*...) while((s32[]{:T(128)}, bf16[2,128,1024]{2,1,0:T(8,128)(2,1)}, ...), condition=%wide.region_5.6_spmd, body=%wide.region_0.5_spmd.sunk | while | flops 303169408 | bytes 10000294 | solution.py:91
  219.7 3.1 %dynamic-slice_bitcast_fusion.4 = bf16[8,128,1024]{2,1,0:T(8,128)(2,1)} fusion(bf16[2,8,128,1024]{3,2,1,0:T(8,128)(2,1)} %get-tuple-element.320, s32[]{:T(128)S(6)} %select_n.45), kind=kLoop, calls=%fused_computation.10.clone.1 | loop fusion | bytes 4194308 | tf_op jit(solution)/shard_map/while/body/eval_jaxpr/squeeze | solution.py:68
  222.8 15.2 %while.24 = (s32[]{:T(128)}, f32[128,1024]{1,0:T(8,128)S(1)}, s32[]{:T(128)}, bf16[8,128,128]{2,1,0:T(8,128)(2,1)S(1)}, bf16[8,128,1024]{2,1,0:T(8,128)(2,1)}, /*index=5*/s32[]{:T(128)}, s32[]{:T(128)}, s32[]{:T(128)}) while((s32[]{:T(128)}, f32[128,1024]{1,0:T(8,128)S(1)}, s32[]{:T(128)}, bf16[8,128,128]{2,1,0:T(8,128)(2,1)S(1)}, ...), condition=%wide.region_2.2_spmd, body=%wide.region_1.1_spmd.sunk | while | flops 33685508 | bytes 1344631 | solution.py:78
  238.1 2.9 %fusion.39 = bf16[2,128,1024]{2,1,0:T(8,128)(2,1)} fusion(bf16[2,128,1024]{2,1,0:T(8,128)(2,1)} %get-tuple-element.301, s32[]{:T(128)} %get-tuple-element.300, f32[128,1024]{1,0:T(8,128)S(1)} %get-tuple-element.233, bf16[2,8,128,1024]{3,2,1,0:T(8,128)(2,1)} %get-tuple-element.322, s32[]{:T(128)S(6)} %select_n.45, f32[128]{0:T(128)S(1)} %add.104, ...), kind=kOutput, calls=%fused_computation.16.clone.1 | convolution fusion | flops 268828672 | bytes 3147776 | tf_op jit(solution)/shard_map/while/body/eval_jaxpr/hij,hjd->id/dot_general | solution.py:81
  245.8 3.1 %dynamic-slice_bitcast_fusion.4 = bf16[8,128,1024]{2,1,0:T(8,128)(2,1)} fusion(bf16[2,8,128,1024]{3,2,1,0:T(8,128)(2,1)} %get-tuple-element.320, s32[]{:T(128)S(6)} %select_n.45), kind=kLoop, calls=%fused_computation.10.clone.1 | loop fusion | bytes 4194308 | tf_op jit(solution)/shard_map/while/body/eval_jaxpr/squeeze | solution.py:68
  248.9 15.2 %while.24 = (s32[]{:T(128)}, f32[128,1024]{1,0:T(8,128)S(1)}, s32[]{:T(128)}, bf16[8,128,128]{2,1,0:T(8,128)(2,1)S(1)}, bf16[8,128,1024]{2,1,0:T(8,128)(2,1)}, /*index=5*/s32[]{:T(128)}, s32[]{:T(128)}, s32[]{:T(128)}) while((s32[]{:T(128)}, f32[128,1024]{1,0:T(8,128)S(1)}, s32[]{:T(128)}, bf16[8,128,128]{2,1,0:T(8,128)(2,1)S(1)}, ...), condition=%wide.region_2.2_spmd, body=%wide.region_1.1_spmd.sunk | while | flops 33685508 | bytes 1344631 | solution.py:78
  264.2 2.9 %fusion.39 = bf16[2,128,1024]{2,1,0:T(8,128)(2,1)} fusion(bf16[2,128,1024]{2,1,0:T(8,128)(2,1)} %get-tuple-element.301, s32[]{:T(128)} %get-tuple-element.300, f32[128,1024]{1,0:T(8,128)S(1)} %get-tuple-element.233, bf16[2,8,128,1024]{3,2,1,0:T(8,128)(2,1)} %get-tuple-element.322, s32[]{:T(128)S(6)} %select_n.45, f32[128]{0:T(128)S(1)} %add.104, ...), kind=kOutput, calls=%fused_computation.16.clone.1 | convolution fusion | flops 268828672 | bytes 3147776 | tf_op jit(solution)/shard_map/while/body/eval_jaxpr/hij,hjd->id/dot_general | solution.py:81
  267.1 2.5 fusion.29
  (95 shorter events, 61.0 us)
Async XLA Ops:
  6.5 260.6 %copy-start = (bf16[1024,1024]{1,0:T(8,128)(2,1)S(1)}, bf16[1024,1024]{1,0:T(8,128)(2,1)}, u32[]{:S(2)}) copy-start(bf16[1024,1024]{1,0:T(8,128)(2,1)} %param.15) | copy-start | bytes 6291460
  6.5 35.4 %copy-start.2 = (bf16[256,1024]{1,0:T(8,128)(2,1)S(1)}, bf16[256,1024]{1,0:T(8,128)(2,1)}, u32[]{:S(2)}) copy-start(bf16[256,1024]{1,0:T(8,128)(2,1)} %param.13) | copy-start | bytes 1572868
  6.5 155.5 %all-gather.2.cloned.1.call-start = ((), (), s32[]{:S(2)}) async-start(), calls=%async_computation | async-start | bytes 13369344 | tf_op jit(solution)/shard_map/all_gather | solution.py:62
  7.3 20.5 %collective-permute-start = (bf16[256,1024]{1,0:T(8,128)(2,1)}, bf16[256,1024]{1,0:T(8,128)(2,1)}, u32[]{:S(2)}, u32[]{:S(2)}) collective-permute-start(bf16[256,1024]{1,0:T(8,128)(2,1)} %param.13), channel_id=1, source_target_pairs={{0,3},{1,4},{2,5},{3,6},{4,7},{5,8},{6,9},{7,10},{8,11},{9,12},{10... | collective-permute-start | bytes 1572872 | tf_op jit(solution)/shard_map/ppermute | solution.py:12
  11.7 22.9 %collective-permute-start.1 = (bf16[256,1024]{1,0:T(8,128)(2,1)}, bf16[256,1024]{1,0:T(8,128)(2,1)}, u32[]{:S(2)}, u32[]{:S(2)}) collective-permute-start(bf16[256,1024]{1,0:T(8,128)(2,1)} %param.13), channel_id=1, source_target_pairs={{0,2},{1,3},{2,4},{3,5},{4,6},{5,7},{6,8},{7,9},{8,10},{9,11},{10,... | collective-permute-start | bytes 1572872 | tf_op jit(solution)/shard_map/ppermute | solution.py:12
  14.2 25.7 %collective-permute-start.2 = (bf16[256,1024]{1,0:T(8,128)(2,1)}, bf16[256,1024]{1,0:T(8,128)(2,1)}, u32[]{:S(2)}, u32[]{:S(2)}) collective-permute-start(bf16[256,1024]{1,0:T(8,128)(2,1)} %param.13), channel_id=1, source_target_pairs={{0,1},{1,2},{2,3},{3,4},{4,5},{5,6},{6,7},{7,8},{8,9},{9,10},{10,1... | collective-permute-start | bytes 1572872 | tf_op jit(solution)/shard_map/ppermute | solution.py:12
  17.1 25.7 %collective-permute-start.3 = (bf16[256,1024]{1,0:T(8,128)(2,1)}, bf16[256,1024]{1,0:T(8,128)(2,1)}, u32[]{:S(2)}, u32[]{:S(2)}) collective-permute-start(bf16[256,1024]{1,0:T(8,128)(2,1)} %param.13), channel_id=1, source_target_pairs={{1,0},{2,1},{3,2},{4,3},{5,4},{6,5},{7,6},{8,7},{9,8},{10,9},{11,1... | collective-permute-start | bytes 1572872 | tf_op jit(solution)/shard_map/ppermute | solution.py:12
  19.0 25.6 %collective-permute-start.4 = (bf16[256,1024]{1,0:T(8,128)(2,1)}, bf16[256,1024]{1,0:T(8,128)(2,1)S(1)}, u32[]{:S(2)}, u32[]{:S(2)}) collective-permute-start(bf16[256,1024]{1,0:T(8,128)(2,1)} %param.13), channel_id=1, source_target_pairs={{2,0},{3,1},{4,2},{5,3},{6,4},{7,5},{8,6},{9,7},{10,8},{11,9},{12,... | collective-permute-start | bytes 1572872 | tf_op jit(solution)/shard_map/ppermute | solution.py:12
  27.7 24.0 %collective-permute-start.5 = (bf16[256,1024]{1,0:T(8,128)(2,1)}, bf16[256,1024]{1,0:T(8,128)(2,1)S(1)}, u32[]{:S(2)}, u32[]{:S(2)}) collective-permute-start(bf16[256,1024]{1,0:T(8,128)(2,1)} %param.13), channel_id=1, source_target_pairs={{3,0},{4,1},{5,2},{6,3},{7,4},{8,5},{9,6},{10,7},{11,8},{12,9},{13... | collective-permute-start | bytes 1572872 | tf_op jit(solution)/shard_map/ppermute | solution.py:12
  210.3 4.5 %copy-start.1 = (bf16[1,2,8,128,128]{4,3,2,1,0:T(8,128)(2,1)S(1)}, bf16[1,2,8,128,128]{4,3,2,1,0:T(8,128)(2,1)}, u32[]{:S(2)}) copy-start(bf16[1,2,8,128,128]{4,3,2,1,0:T(8,128)(2,1)} %param.16) | copy-start | bytes 1572868
  210.3 4.5 %copy-start.3 = (s32[1,2]{1,0:T(1,128)S(1)}, s32[1,2]{1,0:T(1,128)}, u32[]{:S(2)}) copy-start(s32[1,2]{1,0:T(1,128)} %param.18) | copy-start | bytes 28
Sparse Core Ops, SparseCore 0:
  9.4 152.5 all-gather.1
where the time goes:
time: 279 us; the launch traced here: 276 us
  waiting for transfers between devices  120 us (43%)
  local copies, waits for them, and re-layouts  72 us (26%)
  matrix products  27.2 us (10%)
  starting transfers between devices  18.4 us (7%)
  loops' own time  15.4 us (6%)
  between operations  13.5 us (5%)
  other arithmetic  10.2 us (4%)
    all_gather x1, waiting for transfers between devices, body(): lax.all_gather(history, 'grp', axis=0, tiled=True)  105 us
    gather x48, local copies, waits for them, and re-layouts  48.3 us
    dot_general x16, matrix products, add_tile(): jnp.dot(near_tiles[position], near_data[position], preferred_element_type...  18.9 us
    ppermute x6, starting transfers between devices, shifted_2(): lax.ppermute(value, axis, [(source, source + steps) for source in range(i...  18.4 us
    ppermute x6, waiting for transfers between devices, shifted_2(): lax.ppermute(value, axis, [(source, source + steps) for source in range(i...  14.5 us
    another operation x2, loops' own time, block_mean(): lax.fori_loop(0, live_here, add_tile, jnp.zeros((tile_size, feat_width),...  11.5 us
    unnamed x14, local copies, waits for them, and re-layouts  9.24 us
    squeeze x2, local copies, waits for them, and re-layouts, block_mean(): near_data = near_rows[block_index]  6.17 us
  transfers between devices with their start and end apart: 7, of which 5 were waited for; matrix products, arithmetic and copies ran while one was open for 6% of the time, Pallas kernels for 0%

commit v1 on v0

v1 whole, which is shorter than its diff:
```python
import functools

import jax
import jax.numpy as jnp
from jax import lax
from jax.experimental import pallas as pl
from jax.experimental.pallas import tpu as pltpu
from jax.sharding import PartitionSpec as P

MESH = pl.DeviceIdType.MESH
BAND = 6
COLS = 256


def kernel(
    n_grp, n_row, reach,
    cols_ref, live_ref, owner_ref, block_ref,
    feat, hist, weight, near_in, far_in,
    out,
    ring, window, w_buf, near_t, far_t, acc, inv, out_buf,
    load_sem, z_send, z_recv, last_send, last_recv, row_send, row_recv,
):
    g = lax.axis_index("grp")
    r = lax.axis_index("row")
    half = n_grp // 2
    tile = near_t.shape[1]
    width = feat.shape[2]
    blocks = feat.shape[0]
    chunks = hist.shape[0] // tile
    slots = near_t.shape[0] // blocks
    tiles_far = far_t.shape[0] // blocks
    requests = far_t.shape[0]
    shard = hist.shape[0]

    right = lax.rem(g + 1, n_grp)
    left = lax.rem(g + n_grp - 1, n_grp)
    steps = [d for d in range(-reach, reach + 1) if d != 0]

    loads = [
        pltpu.make_async_copy(far_in, far_t, load_sem.at[0]),
        pltpu.make_async_copy(hist, ring.at[0], load_sem.at[1]),
        pltpu.make_async_copy(near_in, near_t, load_sem.at[2]),
        pltpu.make_async_copy(
            feat, window.at[pl.ds(reach * blocks, blocks)], load_sem.at[3]
        ),
        pltpu.make_async_copy(weight, w_buf, load_sem.at[4]),
    ]
    for load in loads:
        load.start()

    barrier = pltpu.get_barrier_semaphore()
    for z in (left, right):
        pl.semaphore_signal(barrier, inc=1, device_id=(z, r), device_id_type=MESH)
    for d in steps:
        pl.semaphore_signal(
            barrier, inc=1, device_id=(g, lax.rem(r + d + n_row, n_row)), device_id_type=MESH
        )
    pl.semaphore_wait(barrier, 2 + len(steps))

    def slot_of(direction, k):
        return k if direction == 0 else half + k

    def chunk_of(direction, c):
        return c if direction == 0 else chunks - 1 - c

    def z_copy(direction, k, c, own=False):
        piece = chunk_of(direction, c)
        rows = pl.ds(piece * tile, tile)
        slot = slot_of(direction, k)
        return pltpu.make_async_remote_copy(
            src_ref=hist.at[rows] if own else ring.at[slot_of(direction, k - 1), rows],
            dst_ref=ring.at[slot, rows],
            send_sem=z_send.at[slot, piece],
            recv_sem=z_recv.at[slot, piece],
            device_id=(right if direction == 0 else left, r),
            device_id_type=MESH,
        )

    def last_pieces(direction):
        first, stop = (0, shard // 2) if direction == 0 else (shard // 2, shard)
        pieces = []
        for c in range(chunks):
            piece = chunk_of(direction, c)
            low, high = max(first, piece * tile), min(stop, piece * tile + tile)
            if low < high:
                pieces.append((c, low, high - low))
        return pieces

    def last_copy(direction, index):
        _, low, size = last_pieces(direction)[index]
        rows = pl.ds(low, size)
        return pltpu.make_async_remote_copy(
            src_ref=ring.at[slot_of(direction, half - 1), rows],
            dst_ref=ring.at[half, rows],
            send_sem=last_send.at[direction, index],
            recv_sem=last_recv.at[direction, index],
            device_id=(right if direction == 0 else left, r),
            device_id_type=MESH,
        )

    def row_copy(d):
        i = steps.index(d)
        return pltpu.make_async_remote_copy(
            src_ref=feat,
            dst_ref=window.at[pl.ds((reach - d) * blocks, blocks)],
            send_sem=row_send.at[i],
            recv_sem=row_recv.at[i],
            device_id=(g, lax.rem(r + d + n_row, n_row)),
            device_id_type=MESH,
        )

    for c in range(chunks):
        for direction in (0, 1):
            z_copy(direction, 1, c, own=True).start()
    for d in steps:
        row_copy(d).start()

    def far_slot(slot, source):
        count = jnp.int32(0)
        first = jnp.int32(0)
        second = jnp.int32(0)
        first_block = jnp.int32(0)
        second_block = jnp.int32(0)
        for h in range(requests):
            named = (owner_ref[h] == source).astype(jnp.int32)
            to_first = named * (count == 0).astype(jnp.int32)
            to_second = named * (count == 1).astype(jnp.int32)
            first = first + to_first * h
            second = second + to_second * h
            first_block = first_block + to_first * block_ref[h]
            second_block = second_block + to_second * block_ref[h]
            count = count + named
        picked = []
        for index, block, least in ((first, first_block, 0), (second, second_block, 1)):
            values = far_t[index].astype(jnp.float32)
            alive = count > least
            parts = []
            for b in range(blocks):
                mine = alive & (index >= b * tiles_far) & (index < (b + 1) * tiles_far)
                parts.append((values * mine.astype(jnp.float32)).astype(jnp.bfloat16))
            picked.append((jnp.concatenate(parts, axis=0), block))
        lhs = jnp.concatenate([part for part, _ in picked], axis=1)

        @pl.loop(0, width // COLS)
        def _(j):
            where = pl.ds(pl.multiple_of(j * COLS, COLS), COLS)
            data = [ring[slot, pl.ds(p * tile, tile), where] for p in range(chunks)]
            taken = []
            for _, block in picked:
                number = jnp.full((tile, COLS), block, jnp.int32)
                value = data[0]
                for p in range(1, chunks):
                    value = jnp.where(number == p, data[p], value)
                taken.append(value)
            rhs = jnp.concatenate(taken, axis=0)
            acc[:, where] += jnp.dot(lhs, rhs, preferred_element_type=jnp.float32)

    def near_block(b):
        live = live_ref[0, b]
        start = (r - reach) * blocks
        rows = pl.ds(b * tile, tile)
        for t in range(0, slots, 2):
            lhs = jnp.concatenate(
                [
                    (
                        near_t[b * slots + u].astype(jnp.float32)
                        * (u < live).astype(jnp.float32)
                    ).astype(jnp.bfloat16)
                    for u in (t, t + 1)
                ],
                axis=1,
            )
            places = [
                jnp.clip(cols_ref[0, b, u] - start, 0, (2 * reach + 1) * blocks - 1)
                for u in (t, t + 1)
            ]

            @pl.loop(0, width // COLS)
            def _(j):
                where = pl.ds(pl.multiple_of(j * COLS, COLS), COLS)
                rhs = jnp.concatenate(
                    [window[p, :, where] for p in places],
                    axis=0,
                )
                acc[rows, where] += jnp.dot(lhs, rhs, preferred_element_type=jnp.float32)

    acc[...] = jnp.zeros_like(acc)
    loads[0].wait()
    loads[1].wait()
    far_slot(0, g)

    loads[2].wait()
    for b in range(blocks):
        live = live_ref[0, b]
        total = jnp.zeros((tile, tile), jnp.float32)
        for t in range(slots):
            total = total + near_t[b * slots + t].astype(jnp.float32) * (t < live).astype(jnp.float32)
        for h in range(tiles_far):
            total = total + far_t[b * tiles_far + h].astype(jnp.float32)
        sums = jnp.sum(total, axis=1, keepdims=True)
        inv[pl.ds(b * tile, tile), :] = jnp.broadcast_to(1.0 / sums, (tile, tile))

    @pl.loop(1, half - 1)
    def _(k):
        for c in range(chunks):
            for direction in (0, 1):
                z_copy(direction, k, c).wait_recv()
                z_copy(direction, k + 1, c).start()
        far_slot(k, lax.rem(g - k + n_grp, n_grp))
        far_slot(half + k, lax.rem(g + k, n_grp))

    k = half - 1
    for c in range(chunks):
        for direction in (0, 1):
            z_copy(direction, k, c).wait_recv()
            for index, (piece, _, _) in enumerate(last_pieces(direction)):
                if piece == c:
                    last_copy(direction, index).start()
    far_slot(k, lax.rem(g - k + n_grp, n_grp))
    far_slot(half + k, lax.rem(g + k, n_grp))

    loads[3].wait()
    for d in steps:
        row_copy(d).wait()
    for b in range(blocks):
        near_block(b)

    for c in range(chunks):
        for direction in (0, 1):
            z_copy(direction, 1, c, own=True).wait_send()

    @pl.loop(1, half - 1)
    def _(k):
        for c in range(chunks):
            for direction in (0, 1):
                z_copy(direction, k + 1, c).wait_send()

    loads[4].wait()
    for direction in (0, 1):
        for index in range(len(last_pieces(direction))):
            last_copy(direction, index).wait()
    far_slot(half, lax.rem(g + half, n_grp))

    mean = (acc[...] * jnp.concatenate([inv[...]] * (width // tile), axis=1)).astype(jnp.bfloat16)
    @pl.loop(0, width // COLS)
    def _(j):
        where = pl.ds(pl.multiple_of(j * COLS, COLS), COLS)
        full = jnp.dot(mean, w_buf[:, where], preferred_element_type=jnp.float32)
        out_buf[:, where] = jnp.maximum(full, 0.0).astype(jnp.bfloat16)
    store = pltpu.make_async_copy(out_buf, out, load_sem.at[0])
    store.start()
    store.wait()


def solution(mesh):
    n_grp, n_row = mesh.shape["grp"], mesh.shape["row"]

    def body(
        features, history, weight, in_tiles, in_cols, tile_live, hist_tiles, hist_owner, hist_block
    ):
        tile = in_tiles.shape[3]
        rows, width = features.shape
        blocks = rows // tile
        shard = history.shape[0]
        chunks = shard // tile
        reach = (BAND + blocks - 1) // blocks
        near = in_tiles.reshape(-1, tile, tile)
        far = hist_tiles.reshape(-1, tile, tile)
        smem = pl.BlockSpec(memory_space=pltpu.SMEM)
        hbm = pl.BlockSpec(memory_space=pl.ANY)
        return pl.pallas_call(
            functools.partial(kernel, n_grp, n_row, reach),
            out_shape=jax.ShapeDtypeStruct((rows, width), jnp.bfloat16),
            in_specs=[smem] * 4 + [hbm] * 5,
            out_specs=hbm,
            scratch_shapes=[
                pltpu.VMEM((n_grp, shard, width), jnp.bfloat16),
                pltpu.VMEM(((2 * reach + 1) * blocks, tile, width), jnp.bfloat16),
                pltpu.VMEM(weight.shape, jnp.bfloat16),
                pltpu.VMEM(near.shape, jnp.bfloat16),
                pltpu.VMEM(far.shape, jnp.bfloat16),
                pltpu.VMEM((rows, width), jnp.float32),
                pltpu.VMEM((rows, tile), jnp.float32),
                pltpu.VMEM((rows, width), jnp.bfloat16),
                pltpu.SemaphoreType.DMA((5,)),
                pltpu.SemaphoreType.DMA((n_grp, chunks)),
                pltpu.SemaphoreType.DMA((n_grp, chunks)),
                pltpu.SemaphoreType.DMA((2, chunks)),
                pltpu.SemaphoreType.DMA((2, chunks)),
                pltpu.SemaphoreType.DMA((2 * reach,)),
                pltpu.SemaphoreType.DMA((2 * reach,)),
            ],
            compiler_params=pltpu.CompilerParams(
                collective_id=0, has_side_effects=True, vmem_limit_bytes=60 * 1024 * 1024
            ),
        )(
            in_cols, tile_live, hist_owner.reshape(-1), hist_block.reshape(-1),
            features.reshape(-1, tile, width), history, weight, near, far,
        )

    placed = (
        P(("grp", "row"), None),
        P(("grp", "row"), None),
        P(),
        P("grp", "row", None, None, None),
        P("grp", "row", None),
        P("grp", "row"),
        P("grp", "row", None, None, None),
        P(("grp", "row"), None),
        P(("grp", "row"), None),
    )
    return jax.shard_map(
        body, mesh=mesh, in_specs=placed, out_specs=P(("grp", "row"), None), check_vma=False
    )
```

time: 279 us -> 151 us (0.54)
  the two profiles are of different devices: /device:TPU:3 before, /device:TPU:1 now
where the time goes in v1:
time: 151 us; the launch traced here: 150 us
  Pallas kernels  148 us (98%)
  local copies, waits for them, and re-layouts  1.87 us (1%)
    pallas_call x1, Pallas kernels, body(): pl.pallas_call(functools.partial(kernel, n_grp, n_row, reach), out_shape=...  148 us

profile of v1, /device:TPU:1, one launch (start us, length us, event | category | flops | bytes accessed | tf_op | source)
XLA Modules:
  0.0 150.4 jit_solution(7283388859527713199)
XLA Ops:
  0.0 148.5 %shard_map.91 = bf16[256,1024]{1,0:T(8,128)(2,1)} custom-call(s32[1,2,8]{2,1,0:T(2,128)} %cols_ref.1, s32[1,2]{1,0:T(1,128)} %live_ref.1, s32[16]{0:T(128)} %bitcast.8, s32[16]{0:T(128)} %bitcast.9, bf16[2,128,1024]{2,1,0:T(8,128)(2,1)} %bitcast.5, bf16[384,1024]{1,0:T(8,128)(2,1)} %hist.1, bf16[1024,1024]{1,0:T(8,128)(2,1)} %weight.1, ...), custom_call_target="tpu_custom_call" | custom-call | tf_op jit(solution)/shard_map/pallas_call | solution.py:271
  148.5 1.9 %copy.11 = bf16[256,1024]{1,0:T(8,128)(2,1)} copy(bf16[256,1024]{1,0:T(8,128)(2,1)} %shard_map.91) | data formatting | bytes 1048576

commit v2 on v1

v2 whole, which is shorter than its diff:
```python
import functools

import jax
import jax.numpy as jnp
from jax import lax
from jax.experimental import pallas as pl
from jax.experimental.pallas import tpu as pltpu
from jax.sharding import PartitionSpec as P

MESH = pl.DeviceIdType.MESH
BAND = 6
COLS = 256


def split_ring(n_grp):
    far = (n_grp - 4) // 4
    ahead = n_grp // 2 - far
    behind = n_grp - 1 - 2 * far - ahead
    return behind, ahead, far


def kernel(
    n_grp, n_row, reach,
    cols_ref, live_ref, owner_ref, block_ref,
    feat, hist, weight, near_in, far_in,
    out,
    ring, window, w_buf, near_t, far_t, acc, inv, mean, out_buf,
    packets, relays, parts, part_send, part_recv,
    load_sem, z_send, z_recv, tile_send, tile_recv, sum_send, sum_recv, row_send, row_recv,
):
    g = lax.axis_index("grp")
    r = lax.axis_index("row")
    behind, ahead, n_far = split_ring(n_grp)
    tile = near_t.shape[1]
    blocks, _, width = feat.shape
    chunks = hist.shape[0] // tile
    slots = near_t.shape[0] // blocks
    tiles_far = far_t.shape[0] // blocks
    requests = far_t.shape[0]
    own = behind
    steps = [d for d in range(-reach, reach + 1) if d != 0]

    sign = 1 - 2 * lax.rem(r, 2)

    def at(distance):
        return lax.rem(g + sign * distance + 2 * n_grp, n_grp)

    def beside(d):
        return lax.rem(r + d + n_row, n_row)

    loads = [
        pltpu.make_async_copy(far_in, far_t, load_sem.at[0]),
        pltpu.make_async_copy(hist, ring.at[own], load_sem.at[1]),
        pltpu.make_async_copy(near_in, near_t, load_sem.at[2]),
        pltpu.make_async_copy(feat, window.at[pl.ds(reach * blocks, blocks)], load_sem.at[3]),
        pltpu.make_async_copy(weight, w_buf, load_sem.at[4]),
    ]
    for load in loads:
        load.start()

    barrier = pltpu.get_barrier_semaphore()
    for j in range(1, n_far + 1):
        for z in (at(-j), at(j)):
            pl.semaphore_signal(barrier, inc=1, device_id=(z, r), device_id_type=MESH)
    for d in steps:
        pl.semaphore_signal(barrier, inc=1, device_id=(g, beside(d)), device_id_type=MESH)
    pl.semaphore_wait(barrier, 2 * n_far + len(steps))

    def slot_of(direction, k):
        return own - k if direction == 0 else own + k

    def towards(direction):
        return at(1) if direction == 0 else at(-1)

    def z_copy(direction, k, c, first=False):
        rows = pl.ds(c * tile, tile)
        slot = slot_of(direction, k)
        return pltpu.make_async_remote_copy(
            src_ref=hist.at[rows] if first else ring.at[slot_of(direction, k - 1), rows],
            dst_ref=ring.at[slot, rows],
            send_sem=z_send.at[slot, c],
            recv_sem=z_recv.at[slot, c],
            device_id=(towards(direction), r),
            device_id_type=MESH,
        )

    def packet_copy(direction, j):
        index = n_far - j if direction == 0 else n_far + own + ahead + j
        return pltpu.make_async_remote_copy(
            src_ref=packets.at[index],
            dst_ref=relays.at[direction, j - 1],
            send_sem=tile_send.at[direction, j - 1],
            recv_sem=tile_recv.at[direction, j - 1],
            device_id=(at(-j) if direction == 0 else at(j), r),
            device_id_type=MESH,
        )

    def sum_copy(direction, h, b):
        return pltpu.make_async_remote_copy(
            src_ref=part_send.at[direction, h - 1, b],
            dst_ref=part_recv.at[direction, h - 1, b],
            send_sem=sum_send.at[direction, h - 1, b],
            recv_sem=sum_recv.at[direction, h - 1, b],
            device_id=(towards(direction), r),
            device_id_type=MESH,
        )

    def row_copy(d):
        i = steps.index(d)
        return pltpu.make_async_remote_copy(
            src_ref=feat,
            dst_ref=window.at[pl.ds((reach - d) * blocks, blocks)],
            send_sem=row_send.at[i],
            recv_sem=row_recv.at[i],
            device_id=(g, beside(d)),
            device_id_type=MESH,
        )

    for c in range(chunks):
        for direction in (0, 1):
            z_copy(direction, 1, c, first=True).start()
    for d in steps:
        row_copy(d).start()

    def pack(i):
        source = at(i - behind - n_far)
        count = jnp.int32(0)
        index = [jnp.int32(0), jnp.int32(0)]
        block = [jnp.int32(0), jnp.int32(0)]
        for h in range(requests):
            named = (owner_ref[h] == source).astype(jnp.int32)
            for c in range(2):
                taken = named * (count == c).astype(jnp.int32)
                index[c] = index[c] + taken * h
                block[c] = block[c] + taken * block_ref[h]
            count = count + named
        marks = []
        for c in range(2):
            alive = (count > c).astype(jnp.float32)
            packets[i, pl.ds(c * tile, tile), :] = (
                far_t[index[c]].astype(jnp.float32) * alive
            ).astype(jnp.bfloat16)
            marks += [index[c] // tiles_far, block[c]]
        row = lax.broadcasted_iota(jnp.int32, (16, tile), 0)
        rows = jnp.zeros((16, tile), jnp.int32)
        for n, mark in enumerate(marks):
            rows = rows + (row == n).astype(jnp.int32) * mark
        packets[i, pl.ds(2 * tile, 16), :] = rows.astype(jnp.float32).astype(jnp.bfloat16)

    def apply(packet, slot, put):
        marks = packet[pl.ds(2 * tile, 16), :].astype(jnp.float32).astype(jnp.int32)
        tops = [[] for _ in range(blocks)]
        numbers = []
        for c in range(2):
            values = packet[pl.ds(c * tile, tile), :].astype(jnp.float32)
            mine = marks[2 * c : 2 * c + 1, :]
            for b in range(blocks):
                keep = (mine == b).astype(jnp.float32)
                tops[b].append((values * keep).astype(jnp.bfloat16))
            numbers.append(
                jnp.broadcast_to(
                    jnp.concatenate([marks[2 * c + 1 : 2 * c + 2, :]] * (COLS // tile), axis=1),
                    (tile, COLS),
                )
            )
        lhs = jnp.concatenate([jnp.concatenate(top, axis=1) for top in tops], axis=0)

        @pl.loop(0, width // COLS)
        def _(j):
            where = pl.ds(pl.multiple_of(j * COLS, COLS), COLS)
            data = [ring[slot, pl.ds(p * tile, tile), where] for p in range(chunks)]
            taken = []
            for number in numbers:
                value = data[0]
                for p in range(1, chunks):
                    value = jnp.where(number == p, data[p], value)
                taken.append(value)
            rhs = jnp.concatenate(taken, axis=0)
            put(where, jnp.dot(lhs, rhs, preferred_element_type=jnp.float32))

    def far_slot(slot):
        def put(where, value):
            acc[:, where] += value

        apply(packets.at[slot + n_far], slot, put)

    def relay_first(direction):
        def put(where, value):
            for b in range(blocks):
                part_send[direction, 0, b, :, where] = value[b * tile : (b + 1) * tile].astype(
                    jnp.bfloat16
                )

        slot = 0 if direction == 0 else own + ahead
        apply(relays.at[direction, n_far - 1], slot, put)
        for b in range(blocks):
            sum_copy(direction, 1, b).start()

    def relay_later(direction):
        for j in range(n_far - 1, 0, -1):
            def put(where, value, j=j):
                parts[direction, j - 1, :, where] = value

            slot = 0 if direction == 0 else own + ahead
            apply(relays.at[direction, j - 1], slot, put)

    def relay_hop(direction, h):
        for b in range(blocks):
            sum_copy(direction, h - 1, b).wait_recv()
            part_send[direction, h - 1, b] = (
                parts[direction, n_far - h, pl.ds(b * tile, tile), :]
                + part_recv[direction, h - 2, b].astype(jnp.float32)
            ).astype(jnp.bfloat16)
            sum_copy(direction, h, b).start()

    def near_block(b):
        live = live_ref[0, b]
        start = (r - reach) * blocks
        rows = pl.ds(b * tile, tile)
        for t in range(0, slots, 2):
            lhs = jnp.concatenate(
                [
                    (
                        near_t[b * slots + u].astype(jnp.float32)
                        * (u < live).astype(jnp.float32)
                    ).astype(jnp.bfloat16)
                    for u in (t, t + 1)
                ],
                axis=1,
            )
            places = [
                jnp.clip(cols_ref[0, b, u] - start, 0, (2 * reach + 1) * blocks - 1)
                for u in (t, t + 1)
            ]

            @pl.loop(0, width // COLS)
            def _(j):
                where = pl.ds(pl.multiple_of(j * COLS, COLS), COLS)
                rhs = jnp.concatenate([window[p, :, where] for p in places], axis=0)
                acc[rows, where] += jnp.dot(lhs, rhs, preferred_element_type=jnp.float32)

    loads[0].wait()

    @pl.loop(0, n_grp)
    def _(i):
        pack(i)

    for j in range(n_far, 0, -1):
        for direction in (0, 1):
            packet_copy(direction, j).start()

    acc[...] = jnp.zeros_like(acc)
    loads[1].wait()
    far_slot(own)

    loads[2].wait()
    for b in range(blocks):
        live = live_ref[0, b]
        total = jnp.zeros((tile, tile), jnp.float32)
        for t in range(slots):
            total = total + near_t[b * slots + t].astype(jnp.float32) * (t < live).astype(jnp.float32)
        for h in range(tiles_far):
            total = total + far_t[b * tiles_far + h].astype(jnp.float32)
        sums = jnp.sum(total, axis=1, keepdims=True)
        inv[pl.ds(b * tile, tile), :] = jnp.broadcast_to(1.0 / sums, (tile, tile))

    both = min(behind, ahead)

    @pl.loop(1, both)
    def _(k):
        for c in range(chunks):
            for direction in (0, 1):
                z_copy(direction, k, c).wait_recv()
                z_copy(direction, k + 1, c).start()
        far_slot(own - k)
        far_slot(own + k)

    for c in range(chunks):
        z_copy(0, both, c).wait_recv()
        z_copy(1, both, c).wait_recv()
        z_copy(1, both + 1, c).start()
    for j in range(1, n_far + 1):
        packet_copy(0, j).wait()
        packet_copy(1, j).wait()
    relay_first(0)
    relay_later(0)
    far_slot(own - both)
    far_slot(own + both)
    loads[3].wait()
    for d in steps:
        row_copy(d).wait()
    for b in range(blocks):
        near_block(b)

    for h in range(2, n_far):
        relay_hop(0, h)
    for c in range(chunks):
        z_copy(1, ahead, c).wait_recv()
    relay_first(1)
    relay_hop(0, n_far)
    relay_later(1)
    far_slot(own + ahead)
    for h in range(2, n_far):
        relay_hop(1, h)
    for b in range(blocks):
        sum_copy(0, n_far, b).wait_recv()
        acc[pl.ds(b * tile, tile), :] += part_recv[0, n_far - 1, b].astype(jnp.float32)
    relay_hop(1, n_far)

    for c in range(chunks):
        for direction in (0, 1):
            z_copy(direction, 1, c, first=True).wait_send()

    @pl.loop(1, both)
    def _(k):
        for c in range(chunks):
            for direction in (0, 1):
                z_copy(direction, k + 1, c).wait_send()

    for c in range(chunks):
        z_copy(1, ahead, c).wait_send()
    for h in range(1, n_far):
        for b in range(blocks):
            sum_copy(0, h, b).wait_send()
            sum_copy(1, h, b).wait_send()
    for b in range(blocks):
        sum_copy(0, n_far, b).wait_send()

    loads[4].wait()
    stores = []
    for b in range(blocks):
        rows = pl.ds(b * tile, tile)
        sum_copy(1, n_far, b).wait_recv()
        scale = jnp.concatenate([inv[rows, :]] * (width // tile), axis=1)
        mean[...] = (
            (acc[rows, :] + part_recv[1, n_far - 1, b].astype(jnp.float32)) * scale
        ).astype(jnp.bfloat16)

        @pl.loop(0, width // COLS)
        def _(j):
            where = pl.ds(pl.multiple_of(j * COLS, COLS), COLS)
            full = jnp.dot(mean[...], w_buf[:, where], preferred_element_type=jnp.float32)
            out_buf[rows, where] = jnp.maximum(full, 0.0).astype(jnp.bfloat16)

        stores.append(pltpu.make_async_copy(out_buf.at[rows], out.at[rows], load_sem.at[b]))
        stores[-1].start()
    for b in range(blocks):
        sum_copy(1, n_far, b).wait_send()
        stores[b].wait()


def solution(mesh):
    n_grp, n_row = mesh.shape["grp"], mesh.shape["row"]

    def body(
        features, history, weight, in_tiles, in_cols, tile_live, hist_tiles, hist_owner, hist_block
    ):
        tile = in_tiles.shape[3]
        rows, width = features.shape
        blocks = rows // tile
        shard = history.shape[0]
        chunks = shard // tile
        reach = (BAND + blocks - 1) // blocks
        behind, ahead, n_far = split_ring(n_grp)
        held = behind + 1 + ahead
        near = in_tiles.reshape(-1, tile, tile)
        far = hist_tiles.reshape(-1, tile, tile)
        smem = pl.BlockSpec(memory_space=pltpu.SMEM)
        hbm = pl.BlockSpec(memory_space=pl.ANY)
        bf16, f32 = jnp.bfloat16, jnp.float32
        dma = pltpu.SemaphoreType.DMA
        packet = 2 * tile + 16
        return pl.pallas_call(
            functools.partial(kernel, n_grp, n_row, reach),
            out_shape=jax.ShapeDtypeStruct((rows, width), bf16),
            in_specs=[smem] * 4 + [hbm] * 5,
            out_specs=hbm,
            scratch_shapes=[
                pltpu.VMEM((held, shard, width), bf16),
                pltpu.VMEM(((2 * reach + 1) * blocks, tile, width), bf16),
                pltpu.VMEM(weight.shape, bf16),
                pltpu.VMEM(near.shape, bf16),
                pltpu.VMEM(far.shape, bf16),
                pltpu.VMEM((rows, width), f32),
                pltpu.VMEM((rows, tile), f32),
                pltpu.VMEM((tile, width), bf16),
                pltpu.VMEM((rows, width), bf16),
                pltpu.VMEM((n_grp, packet, tile), bf16),
                pltpu.VMEM((2, n_far, packet, tile), bf16),
                pltpu.VMEM((2, n_far - 1, rows, width), f32),
                pltpu.VMEM((2, n_far, blocks, tile, width), bf16),
                pltpu.VMEM((2, n_far, blocks, tile, width), bf16),
                dma((5,)),
                dma((held, chunks)),
                dma((held, chunks)),
                dma((2, n_far)),
                dma((2, n_far)),
                dma((2, n_far, blocks)),
                dma((2, n_far, blocks)),
                dma((2 * reach,)),
                dma((2 * reach,)),
            ],
            compiler_params=pltpu.CompilerParams(
                collective_id=0, has_side_effects=True, vmem_limit_bytes=60 * 1024 * 1024
            ),
        )(
            in_cols, tile_live, hist_owner.reshape(-1), hist_block.reshape(-1),
            features.reshape(-1, tile, width), history, weight, near, far,
        )

    placed = (
        P(("grp", "row"), None),
        P(("grp", "row"), None),
        P(),
        P("grp", "row", None, None, None),
        P("grp", "row", None),
        P("grp", "row"),
        P("grp", "row", None, None, None),
        P(("grp", "row"), None),
        P(("grp", "row"), None),
    )
    return jax.shard_map(
        body, mesh=mesh, in_specs=placed, out_specs=P(("grp", "row"), None), check_vma=False
    )
```

time: 151 us -> 142 us (0.940)
  Pallas kernels: 148 us -> 140 us
    pallas_call x1, Pallas kernels: 148 us -> 140 us  [body(): pl.pallas_call(functools.partial(kernel, n_grp, n_row, reach), out_shape=...]
where the time goes in v2:
time: 142 us; the launch traced here: 141 us
  Pallas kernels  140 us (99%)
  local copies, waits for them, and re-layouts  1.87 us (1%)
    pallas_call x1, Pallas kernels, body(): pl.pallas_call(functools.partial(kernel, n_grp, n_row, reach), out_shape=...  140 us

profile of v2, /device:TPU:1, one launch (start us, length us, event | category | flops | bytes accessed | tf_op | source)
XLA Modules:
  0.0 141.4 jit_solution(17182453974117368300)
XLA Ops:
  0.0 139.5 %shard_map.91 = bf16[256,1024]{1,0:T(8,128)(2,1)} custom-call(s32[1,2,8]{2,1,0:T(2,128)} %cols_ref.1, s32[1,2]{1,0:T(1,128)} %live_ref.1, s32[16]{0:T(128)} %bitcast.8, s32[16]{0:T(128)} %bitcast.9, bf16[2,128,1024]{2,1,0:T(8,128)(2,1)} %bitcast.5, bf16[384,1024]{1,0:T(8,128)(2,1)} %hist.1, bf16[1024,1024]{1,0:T(8,128)(2,1)} %weight.1, ...), custom_call_target="tpu_custom_call" | custom-call | tf_op jit(solution)/shard_map/pallas_call | solution.py:373
  139.5 1.9 %copy.11 = bf16[256,1024]{1,0:T(8,128)(2,1)} copy(bf16[256,1024]{1,0:T(8,128)(2,1)} %shard_map.91) | data formatting | bytes 1048576

commit v3 on v2

--- a/solution.py
+++ b/solution.py
@@ -12,25 +12,28 @@
 COLS = 256
 
 
+BEHIND, AHEAD, FAR_AHEAD = 4, 5, 3
+PIECE = 128
+
+
 def split_ring(n_grp):
-    far = (n_grp - 4) // 4
-    ahead = n_grp // 2 - far
-    behind = n_grp - 1 - 2 * far - ahead
-    return behind, ahead, far
+    far = n_grp - 1 - BEHIND - AHEAD
+    return (BEHIND, AHEAD), (far - FAR_AHEAD, FAR_AHEAD)
 
 
 def kernel(
     n_grp, n_row, reach,
     cols_ref, live_ref, owner_ref, block_ref,
-    feat, hist, weight, near_in, far_in,
+    feat, hist, near_in, far_in,
     out,
-    ring, window, w_buf, near_t, far_t, acc, inv, mean, out_buf,
+    ring, window, near_t, far_t, acc, inv,
     packets, relays, parts, part_send, part_recv,
     load_sem, z_send, z_recv, tile_send, tile_recv, sum_send, sum_recv, row_send, row_recv,
 ):
     g = lax.axis_index("grp")
     r = lax.axis_index("row")
-    behind, ahead, n_far = split_ring(n_grp)
+    reached, n_far = split_ring(n_grp)
+    behind, ahead = reached
     tile = near_t.shape[1]
     blocks, _, width = feat.shape
     chunks = hist.shape[0] // tile
@@ -38,6 +41,7 @@
     tiles_far = far_t.shape[0] // blocks
     requests = far_t.shape[0]
     own = behind
+    pieces = acc.shape[0] // PIECE
     steps = [d for d in range(-reach, reach + 1) if d != 0]
 
     sign = 1 - 2 * lax.rem(r, 2)
@@ -53,18 +57,18 @@
         pltpu.make_async_copy(hist, ring.at[own], load_sem.at[1]),
         pltpu.make_async_copy(near_in, near_t, load_sem.at[2]),
         pltpu.make_async_copy(feat, window.at[pl.ds(reach * blocks, blocks)], load_sem.at[3]),
-        pltpu.make_async_copy(weight, w_buf, load_sem.at[4]),
     ]
     for load in loads:
         load.start()
 
     barrier = pltpu.get_barrier_semaphore()
-    for j in range(1, n_far + 1):
+    partners = max(n_far)
+    for j in range(1, partners + 1):
         for z in (at(-j), at(j)):
             pl.semaphore_signal(barrier, inc=1, device_id=(z, r), device_id_type=MESH)
     for d in steps:
         pl.semaphore_signal(barrier, inc=1, device_id=(g, beside(d)), device_id_type=MESH)
-    pl.semaphore_wait(barrier, 2 * n_far + len(steps))
+    pl.semaphore_wait(barrier, 2 * partners + len(steps))
 
     def slot_of(direction, k):
         return own - k if direction == 0 else own + k
@@ -85,7 +89,7 @@
         )
 
     def packet_copy(direction, j):
-        index = n_far - j if direction == 0 else n_far + own + ahead + j
+        index = n_far[0] - j if direction == 0 else n_far[0] + own + ahead + j
         return pltpu.make_async_remote_copy(
             src_ref=packets.at[index],
             dst_ref=relays.at[direction, j - 1],
@@ -95,12 +99,13 @@
             device_id_type=MESH,
         )
 
-    def sum_copy(direction, h, b):
+    def sum_copy(direction, h, p):
+        rows = pl.ds(p * PIECE, PIECE)
         return pltpu.make_async_remote_copy(
-            src_ref=part_send.at[direction, h - 1, b],
-            dst_ref=part_recv.at[direction, h - 1, b],
-            send_sem=sum_send.at[direction, h - 1, b],
-            recv_sem=sum_recv.at[direction, h - 1, b],
+            src_ref=part_send.at[direction, h - 1, rows],
+            dst_ref=part_recv.at[direction, h - 1, rows],
+            send_sem=sum_send.at[direction, h - 1, p],
+            recv_sem=sum_recv.at[direction, h - 1, p],
             device_id=(towards(direction), r),
             device_id_type=MESH,
         )
@@ -123,7 +128,7 @@
         row_copy(d).start()
 
     def pack(i):
-        source = at(i - behind - n_far)
+        source = at(i - behind - n_far[0])
         count = jnp.int32(0)
         index = [jnp.int32(0), jnp.int32(0)]
         block = [jnp.int32(0), jnp.int32(0)]
@@ -182,36 +187,38 @@
         def put(where, value):
             acc[:, where] += value
 
-        apply(packets.at[slot + n_far], slot, put)
+        apply(packets.at[slot + n_far[0]], slot, put)
+
+    def relay_slot(direction):
+        return 0 if direction == 0 else own + ahead
 
     def relay_first(direction):
         def put(where, value):
-            for b in range(blocks):
-                part_send[direction, 0, b, :, where] = value[b * tile : (b + 1) * tile].astype(
-                    jnp.bfloat16
-                )
-
-        slot = 0 if direction == 0 else own + ahead
-        apply(relays.at[direction, n_far - 1], slot, put)
-        for b in range(blocks):
-            sum_copy(direction, 1, b).start()
-
-    def relay_later(direction):
-        for j in range(n_far - 1, 0, -1):
-            def put(where, value, j=j):
-                parts[direction, j - 1, :, where] = value
-
-            slot = 0 if direction == 0 else own + ahead
-            apply(relays.at[direction, j - 1], slot, put)
-
-    def relay_hop(direction, h):
-        for b in range(blocks):
-            sum_copy(direction, h - 1, b).wait_recv()
-            part_send[direction, h - 1, b] = (
-                parts[direction, n_far - h, pl.ds(b * tile, tile), :]
-                + part_recv[direction, h - 2, b].astype(jnp.float32)
+            part_send[direction, 0, :, where] = value.astype(jnp.bfloat16)
+
+        for j in range(1, n_far[direction] + 1):
+            packet_copy(direction, j).wait()
+        apply(relays.at[direction, n_far[direction] - 1], relay_slot(direction), put)
+        for p in range(pieces):
+            sum_copy(direction, 1, p).start()
+
+    def relay_part(direction, j):
+        def put(where, value):
+            parts[direction, j - 1, :, where] = value
+
+        apply(relays.at[direction, j - 1], relay_slot(direction), put)
+
+    def take_hop(direction, h, p):
+        rows = pl.ds(p * PIECE, PIECE)
+        sum_copy(direction, h, p).wait_recv()
+        came = part_recv[direction, h - 1, rows].astype(jnp.float32)
+        if h < n_far[direction]:
+            part_send[direction, h, rows] = (
+                parts[direction, n_far[direction] - h - 1, rows, :] + came
             ).astype(jnp.bfloat16)
-            sum_copy(direction, h, b).start()
+            sum_copy(direction, h + 1, p).start()
+        else:
+            acc[rows, :] += came
 
     def near_block(b):
         live = live_ref[0, b]
@@ -245,9 +252,10 @@
     def _(i):
         pack(i)
 
-    for j in range(n_far, 0, -1):
+    for j in range(partners, 0, -1):
         for direction in (0, 1):
-            packet_copy(direction, j).start()
+            if j <= n_far[direction]:
+                packet_copy(direction, j).start()
 
     acc[...] = jnp.zeros_like(acc)
     loads[1].wait()
@@ -275,37 +283,49 @@
         far_slot(own - k)
         far_slot(own + k)
 
-    for c in range(chunks):
-        z_copy(0, both, c).wait_recv()
-        z_copy(1, both, c).wait_recv()
-        z_copy(1, both + 1, c).start()
-    for j in range(1, n_far + 1):
-        packet_copy(0, j).wait()
-        packet_copy(1, j).wait()
-    relay_first(0)
-    relay_later(0)
-    far_slot(own - both)
-    far_slot(own + both)
     loads[3].wait()
     for d in steps:
         row_copy(d).wait()
     for b in range(blocks):
         near_block(b)
 
-    for h in range(2, n_far):
-        relay_hop(0, h)
-    for c in range(chunks):
-        z_copy(1, ahead, c).wait_recv()
-    relay_first(1)
-    relay_hop(0, n_far)
-    relay_later(1)
-    far_slot(own + ahead)
-    for h in range(2, n_far):
-        relay_hop(1, h)
-    for b in range(blocks):
-        sum_copy(0, n_far, b).wait_recv()
-        acc[pl.ds(b * tile, tile), :] += part_recv[0, n_far - 1, b].astype(jnp.float32)
-    relay_hop(1, n_far)
+    events = {}
+    begin = [n_far[1 - d] * (n_far[1 - d] + 1) for d in (0, 1)]
+    for direction in (0, 1):
+        for k in range(both, reached[direction] + 1):
+            events.setdefault(begin[direction] + 24 * k, []).append((direction, "shard", k))
+        for h in range(1, n_far[direction] + 1):
+            events.setdefault(
+                begin[direction] + 24 * reached[direction] + 16 * h, []
+            ).append((direction, "sum", h))
+    ends = [begin[d] + 24 * reached[d] + 16 * n_far[d] for d in (0, 1)]
+    last = 0 if ends[0] > ends[1] else 1
+    parts_left = {0: [], 1: []}
+    slots_left = []
+    for when in sorted(events):
+        shards = [(d, n) for d, kind, n in events[when] if kind == "shard"]
+        sums = [(d, n) for d, kind, n in events[when] if kind == "sum"]
+        for c in range(chunks):
+            for d, k in shards:
+                z_copy(d, k, c).wait_recv()
+                if k < reached[d]:
+                    z_copy(d, k + 1, c).start()
+        for d, k in shards:
+            if k == reached[d]:
+                relay_first(d)
+                parts_left[d] = list(range(n_far[d] - 1, 0, -1))
+            slots_left.append(slot_of(d, k))
+        for p in range(pieces):
+            for d, h in sums:
+                if (d, h) != (last, n_far[last]):
+                    take_hop(d, h, p)
+        for d in (0, 1):
+            if parts_left[d]:
+                relay_part(d, parts_left[d].pop(0))
+        if slots_left:
+            far_slot(slots_left.pop(0))
+    for slot in slots_left:
+        far_slot(slot)
 
     for c in range(chunks):
         for direction in (0, 1):
@@ -317,36 +337,24 @@
             for direction in (0, 1):
                 z_copy(direction, k + 1, c).wait_send()
 
-    for c in range(chunks):
-        z_copy(1, ahead, c).wait_send()
-    for h in range(1, n_far):
-        for b in range(blocks):
-            sum_copy(0, h, b).wait_send()
-            sum_copy(1, h, b).wait_send()
-    for b in range(blocks):
-        sum_copy(0, n_far, b).wait_send()
-
-    loads[4].wait()
-    stores = []
-    for b in range(blocks):
-        rows = pl.ds(b * tile, tile)
-        sum_copy(1, n_far, b).wait_recv()
+    for direction in (0, 1):
+        for k in range(both, reached[direction]):
+            for c in range(chunks):
+                z_copy(direction, k + 1, c).wait_send()
+        for h in range(1, n_far[direction] + 1):
+            if (direction, h) != (last, n_far[last]):
+                for p in range(pieces):
+                    sum_copy(direction, h, p).wait_send()
+
+    for p in range(pieces):
+        rows = pl.ds(p * PIECE, PIECE)
+        sum_copy(last, n_far[last], p).wait_recv()
         scale = jnp.concatenate([inv[rows, :]] * (width // tile), axis=1)
-        mean[...] = (
-            (acc[rows, :] + part_recv[1, n_far - 1, b].astype(jnp.float32)) * scale
+        out[rows, :] = (
+            (acc[rows, :] + part_recv[last, n_far[last] - 1, rows].astype(jnp.float32)) * scale
         ).astype(jnp.bfloat16)
-
-        @pl.loop(0, width // COLS)
-        def _(j):
-            where = pl.ds(pl.multiple_of(j * COLS, COLS), COLS)
-            full = jnp.dot(mean[...], w_buf[:, where], preferred_element_type=jnp.float32)
-            out_buf[rows, where] = jnp.maximum(full, 0.0).astype(jnp.bfloat16)
-
-        stores.append(pltpu.make_async_copy(out_buf.at[rows], out.at[rows], load_sem.at[b]))
-        stores[-1].start()
-    for b in range(blocks):
-        sum_copy(1, n_far, b).wait_send()
-        stores[b].wait()
+    for p in range(pieces):
+        sum_copy(last, n_far[last], p).wait_send()
 
 
 def solution(mesh):
@@ -361,8 +369,10 @@
         shard = history.shape[0]
         chunks = shard // tile
         reach = (BAND + blocks - 1) // blocks
-        behind, ahead, n_far = split_ring(n_grp)
-        held = behind + 1 + ahead
+        reached, n_far = split_ring(n_grp)
+        most = max(n_far)
+        held = sum(reached) + 1
+        pieces = rows // PIECE
         near = in_tiles.reshape(-1, tile, tile)
         far = hist_tiles.reshape(-1, tile, tile)
         smem = pl.BlockSpec(memory_space=pltpu.SMEM)
@@ -370,43 +380,45 @@
         bf16, f32 = jnp.bfloat16, jnp.float32
         dma = pltpu.SemaphoreType.DMA
         packet = 2 * tile + 16
-        return pl.pallas_call(
+        kept = [
+            pltpu.with_memory_space_constraint(x, pltpu.HBM)
+            for x in (
+                in_cols, tile_live, hist_owner.reshape(-1), hist_block.reshape(-1),
+                features.reshape(-1, tile, width), history, near, far,
+            )
+        ]
+        means = pl.pallas_call(
             functools.partial(kernel, n_grp, n_row, reach),
-            out_shape=jax.ShapeDtypeStruct((rows, width), bf16),
-            in_specs=[smem] * 4 + [hbm] * 5,
-            out_specs=hbm,
+            out_shape=pltpu.VMEM((rows, width), bf16),
+            in_specs=[smem] * 4 + [hbm] * 4,
+            out_specs=pl.BlockSpec(memory_space=pltpu.VMEM),
             scratch_shapes=[
                 pltpu.VMEM((held, shard, width), bf16),
                 pltpu.VMEM(((2 * reach + 1) * blocks, tile, width), bf16),
-                pltpu.VMEM(weight.shape, bf16),
                 pltpu.VMEM(near.shape, bf16),
                 pltpu.VMEM(far.shape, bf16),
                 pltpu.VMEM((rows, width), f32),
                 pltpu.VMEM((rows, tile), f32),
-                pltpu.VMEM((tile, width), bf16),
-                pltpu.VMEM((rows, width), bf16),
                 pltpu.VMEM((n_grp, packet, tile), bf16),
-                pltpu.VMEM((2, n_far, packet, tile), bf16),
-                pltpu.VMEM((2, n_far - 1, rows, width), f32),
-                pltpu.VMEM((2, n_far, blocks, tile, width), bf16),
-                pltpu.VMEM((2, n_far, blocks, tile, width), bf16),
-                dma((5,)),
+                pltpu.VMEM((2, most, packet, tile), bf16),
+                pltpu.VMEM((2, most - 1, rows, width), f32),
+                pltpu.VMEM((2, most, rows, width), bf16),
+                pltpu.VMEM((2, most, rows, width), bf16),
+                dma((4,)),
                 dma((held, chunks)),
                 dma((held, chunks)),
-                dma((2, n_far)),
-                dma((2, n_far)),
-                dma((2, n_far, blocks)),
-                dma((2, n_far, blocks)),
+                dma((2, most)),
+                dma((2, most)),
+                dma((2, most, pieces)),
+                dma((2, most, pieces)),
                 dma((2 * reach,)),
                 dma((2 * reach,)),
             ],
             compiler_params=pltpu.CompilerParams(
-                collective_id=0, has_side_effects=True, vmem_limit_bytes=60 * 1024 * 1024
+                collective_id=0, has_side_effects=True, vmem_limit_bytes=48 * 1024 * 1024
             ),
-        )(
-            in_cols, tile_live, hist_owner.reshape(-1), hist_block.reshape(-1),
-            features.reshape(-1, tile, width), history, weight, near, far,
-        )
+        )(*kept)
+        return jax.nn.relu(jnp.dot(means, weight, preferred_element_type=f32)).astype(bf16)
 
     placed = (
         P(("grp", "row"), None),

time: 142 us -> 140 us (0.986)
  Pallas kernels: 140 us -> 138 us
  local copies, waits for them, and re-layouts: 1.87 us -> 0.01 us
  matrix products: 0 us -> 1.51 us
    unnamed x1 -> x2, local copies, waits for them, and re-layouts: 1.87 us -> 0.01 us
    pallas_call x1, Pallas kernels: 140 us -> 138 us  [body(): pl.pallas_call(functools.partial(kernel, n_grp, n_row, reach), out_shape=...]
    dot_general x0 -> x1, matrix products: none -> 1.51 us  [body(): jnp.dot(means, weight, preferred_element_type=f32)]
where the time goes in v3:
time: 140 us; the launch traced here: 139 us
  Pallas kernels  138 us (99%)
  matrix products  1.51 us (1%)
    pallas_call x1, Pallas kernels, body(): pl.pallas_call(functools.partial(kernel, n_grp, n_row, reach), out_shape=...  138 us

profile of v3, /device:TPU:1, one launch (start us, length us, event | category | flops | bytes accessed | tf_op | source)
XLA Modules:
  0.0 139.5 jit_solution(1874864189156163967)
XLA Ops:
  0.0 0.0 copy-start
  0.0 137.9 %shard_map.91 = bf16[256,1024]{1,0:T(8,128)(2,1)S(1)} custom-call(s32[1,2,8]{2,1,0:T(2,128)} %cols_ref.1, s32[1,2]{1,0:T(1,128)} %live_ref.1, s32[16]{0:T(128)} %bitcast.10, s32[16]{0:T(128)} %bitcast.11, bf16[2,128,1024]{2,1,0:T(8,128)(2,1)} %bitcast.7, bf16[384,1024]{1,0:T(8,128)(2,1)} %hist.1, bf16[16,128,128]{2,1,0:T(8,128)(2,1)} %bitcast.8, ...), custom_call_target="tpu_custom_call" | custom-call | tf_op jit(solution)/shard_map/pallas_call | solution.py:390
  137.9 0.0 copy-done
  137.9 1.5 %fusion = bf16[256,1024]{1,0:T(8,128)(2,1)} fusion(bf16[256,1024]{1,0:T(8,128)(2,1)S(1)} %shard_map.91, bf16[1024,1024]{1,0:T(8,128)(2,1)S(1)} %copy-done), kind=kOutput, calls=%fused_computation.1 | convolution fusion | flops 537395200 | bytes 3145728 | tf_op jit(solution)/shard_map/dot_general | solution.py:421
Async XLA Ops:
  0.0 137.9 %copy-start = (bf16[1024,1024]{1,0:T(8,128)(2,1)S(1)}, bf16[1024,1024]{1,0:T(8,128)(2,1)}, u32[]{:S(2)}) copy-start(bf16[1024,1024]{1,0:T(8,128)(2,1)} %param.11) | copy-start | bytes 6291460

commit v4 on v3

--- a/solution.py
+++ b/solution.py
@@ -23,12 +23,13 @@
 
 def kernel(
     n_grp, n_row, reach,
-    cols_ref, live_ref, owner_ref, block_ref,
+    cols_in, live_in, owner_in, block_in,
     feat, hist, near_in, far_in,
     out,
+    cols_ref, live_ref, owner_ref, block_ref,
     ring, window, near_t, far_t, acc, inv,
     packets, relays, parts, part_send, part_recv,
-    load_sem, z_send, z_recv, tile_send, tile_recv, sum_send, sum_recv, row_send, row_recv,
+    load_sem, table_sem, z_send, z_recv, tile_send, tile_recv, sum_send, sum_recv, row_send, row_recv,
 ):
     g = lax.axis_index("grp")
     r = lax.axis_index("row")
@@ -58,8 +59,12 @@
         pltpu.make_async_copy(near_in, near_t, load_sem.at[2]),
         pltpu.make_async_copy(feat, window.at[pl.ds(reach * blocks, blocks)], load_sem.at[3]),
     ]
-    for load in loads:
-        load.start()
+    tables = [
+        pltpu.make_async_copy(source, table, table_sem.at[i])
+        for i, (source, table) in enumerate(
+            ((owner_in, owner_ref), (block_in, block_ref), (live_in, live_ref), (cols_in, cols_ref))
+        )
+    ]
 
     barrier = pltpu.get_barrier_semaphore()
     partners = max(n_far)
@@ -124,6 +129,8 @@
     for c in range(chunks):
         for direction in (0, 1):
             z_copy(direction, 1, c, first=True).start()
+    for load in loads + tables:
+        load.start()
     for d in steps:
         row_copy(d).start()
 
@@ -247,6 +254,8 @@
                 acc[rows, where] += jnp.dot(lhs, rhs, preferred_element_type=jnp.float32)
 
     loads[0].wait()
+    for table in tables:
+        table.wait()
 
     @pl.loop(0, n_grp)
     def _(i):
@@ -375,7 +384,6 @@
         pieces = rows // PIECE
         near = in_tiles.reshape(-1, tile, tile)
         far = hist_tiles.reshape(-1, tile, tile)
-        smem = pl.BlockSpec(memory_space=pltpu.SMEM)
         hbm = pl.BlockSpec(memory_space=pl.ANY)
         bf16, f32 = jnp.bfloat16, jnp.float32
         dma = pltpu.SemaphoreType.DMA
@@ -390,9 +398,10 @@
         means = pl.pallas_call(
             functools.partial(kernel, n_grp, n_row, reach),
             out_shape=pltpu.VMEM((rows, width), bf16),
-            in_specs=[smem] * 4 + [hbm] * 4,
+            in_specs=[hbm] * 8,
             out_specs=pl.BlockSpec(memory_space=pltpu.VMEM),
             scratch_shapes=[
+                *[pltpu.SMEM(x.shape, jnp.int32) for x in kept[:4]],
                 pltpu.VMEM((held, shard, width), bf16),
                 pltpu.VMEM(((2 * reach + 1) * blocks, tile, width), bf16),
                 pltpu.VMEM(near.shape, bf16),
@@ -404,6 +413,7 @@
                 pltpu.VMEM((2, most - 1, rows, width), f32),
                 pltpu.VMEM((2, most, rows, width), bf16),
                 pltpu.VMEM((2, most, rows, width), bf16),
+                dma((4,)),
                 dma((4,)),
                 dma((held, chunks)),
                 dma((held, chunks)),

time: 140 us -> 139 us (level)
  no operation moved by 1% of the time
where the time goes in v4:
time: 139 us
  Pallas kernels  137 us (99%)
  matrix products  1.51 us (1%)
    pallas_call x1, Pallas kernels, body(): pl.pallas_call(functools.partial(kernel, n_grp, n_row, reach), out_shape=...  137 us

profile of v4, /device:TPU:1, one launch (start us, length us, event | category | flops | bytes accessed | tf_op | source)
XLA Modules:
  0.0 138.8 jit_solution(6487478980611002028)
XLA Ops:
  0.0 0.0 copy-start
  0.0 137.3 %shard_map.91 = bf16[256,1024]{1,0:T(8,128)(2,1)S(1)} custom-call(s32[1,2,8]{2,1,0:T(2,128)} %cols_in.1, s32[1,2]{1,0:T(1,128)} %live_in.1, s32[16]{0:T(128)} %bitcast.10, s32[16]{0:T(128)} %bitcast.11, bf16[2,128,1024]{2,1,0:T(8,128)(2,1)} %bitcast.7, bf16[384,1024]{1,0:T(8,128)(2,1)} %hist.1, bf16[16,128,128]{2,1,0:T(8,128)(2,1)} %bitcast.8, ...), custom_call_target="tpu_custom_call" | custom-call | tf_op jit(solution)/shard_map/pallas_call | solution.py:398
  137.3 0.0 copy-done
  137.3 1.5 %fusion = bf16[256,1024]{1,0:T(8,128)(2,1)} fusion(bf16[256,1024]{1,0:T(8,128)(2,1)S(1)} %shard_map.91, bf16[1024,1024]{1,0:T(8,128)(2,1)S(1)} %copy-done), kind=kOutput, calls=%fused_computation.1 | convolution fusion | flops 537395200 | bytes 3145728 | tf_op jit(solution)/shard_map/dot_general | solution.py:431
Async XLA Ops:
  0.0 137.3 %copy-start = (bf16[1024,1024]{1,0:T(8,128)(2,1)S(1)}, bf16[1024,1024]{1,0:T(8,128)(2,1)}, u32[]{:S(2)}) copy-start(bf16[1024,1024]{1,0:T(8,128)(2,1)} %param.11) | copy-start | bytes 6291460
